TPU v7x, 32 devices: a whole 2x2x4 slice. The times are simulated.
32 devices in a mesh: row: 4 (over y, x), col: 8 (over z, core).
Axes of the slice: x: 2, y: 2, z: 4, core: 2. Of those that a mesh axis runs over, the one named last changes fastest.
Arguments:
- ham_tiles: float32 [4, 8, 320, 128, 128], P('row', 'col'), may hold values from -0.0625 to 0.0625
- tile_list: int32 [4, 8, 320, 2], P('row', 'col'), may hold values from 0 to 31, as said below
- tile_count: int32 [4, 8], P('row', 'col'), may hold values from 1 to 320, as said below
- basis_block: float32 [16, 16384], P(None, ('row', 'col')), may hold values from -6 to 6
- residual_block: float32 [16, 16384], P(None, ('row', 'col')), may hold values from -6 to 6
Outputs:
- h_basis: float32 [16, 16384], P(None, ('row', 'col'))
- h_residual: float32 [16, 16384], P(None, ('row', 'col'))
Inputs may be any that keep to these rules, and one draw needn't show every extreme that they name: `tile_list`: entry 0 is a block row within the grid row, below 32; entry 1 a block column within the grid column, below 16. Live slots name distinct blocks with global row block at most the global column block; slots past the count name arbitrary blocks in range. `tile_count`: each device's count lies between half and all of its share of 320 in proportion to its upper-triangle slots, never above its distinct upper blocks; devices with the most upper-triangle slots hold exactly 320.
All inputs are finite; a program needn't handle non-finite values.
Results may differ from a plain program's by a relative error of at most 0.0003.
Values sent between devices are 32-bit elements; how exact they have to be, the bound alone decides.
No kernel may reach another device: no remote copies, remote signals or barrier semaphores. Data moves between devices by JAX's collectives and lax.ppermute only.
A program may use at most 128 MiB of HBM per device.

v0:
```python
import functools

import jax
import jax.numpy as jnp
from jax import lax
from jax.experimental import pallas as pl
from jax.experimental.pallas import tpu as pltpu
from jax.sharding import PartitionSpec as P

GROUP = 32
LONG_GROUP = 64
MIB = 1024 * 1024
VMEM = pl.BlockSpec(memory_space=pltpu.VMEM)
SMEM = pl.BlockSpec(memory_space=pltpu.SMEM)
ANY = pl.BlockSpec(memory_space=pl.ANY)


def small(kernel, out_shape, name, *args, in_specs=None):
    single = not isinstance(out_shape, list)
    return pl.pallas_call(
        kernel,
        out_shape=out_shape,
        in_specs=in_specs or [VMEM] * len(args),
        out_specs=VMEM if single else [VMEM] * len(out_shape),
        compiler_params=pltpu.CompilerParams(vmem_limit_bytes=2 * MIB),
        name=name,
    )(*args)


def f32(*shape):
    return jax.ShapeDtypeStruct(shape, jnp.float32)


def pass_kernel(in_ref, out_ref):
    out_ref[...] = in_ref[...]


def gather_kernel(*refs):
    *ins, out_ref = refs
    for q, ref in enumerate(reversed(ins)):
        out_ref[q] = ref[...]


def split(x):
    high = x.astype(jnp.bfloat16)
    low = (x - high.astype(jnp.float32)).astype(jnp.bfloat16)
    return high, low


def turned_vectors(x, vecs_ref, at, weight=1.0):
    width, side = x.shape
    high = x.astype(jnp.bfloat16).astype(jnp.float32)
    both = jnp.concatenate([high, x - high] * (side // (2 * width)), axis=0).T * weight
    column = lax.broadcasted_iota(jnp.int32, both.shape, 1)
    vecs_ref[0, at] = jnp.where(column < side // 2, both, 0.0).astype(jnp.bfloat16)
    vecs_ref[1, at] = jnp.where(column < side // 2, 0.0, both).astype(jnp.bfloat16)


def plain_vectors(x, vecs_ref, at, weight=1.0):
    high = x.astype(jnp.bfloat16).astype(jnp.float32)
    vecs_ref[0, at] = (jnp.concatenate([high, x - high], axis=0) * weight).astype(jnp.bfloat16)


def prepare(store, origins, pieces, vecs_ref):
    side = vecs_ref.shape[-1]
    per_piece = pieces[0].shape[1] // side
    blocks = len(pieces) * per_piece
    for s, (origin, piece) in enumerate(zip(origins, pieces)):
        for b in range(per_piece):
            x = piece[:, b * side:(b + 1) * side]
            store(x, vecs_ref, origin * per_piece + b)
            if s == 0:
                store(x, vecs_ref, blocks + b, 0.5)
    for form in range(vecs_ref.shape[0]):
        vecs_ref[form, blocks + per_piece] = jnp.zeros_like(vecs_ref[0, 0])


def shifted(steps, n):
    return lax.rem(lax.axis_index("col") + steps % n, n)


def find_slot(forward, per_piece, t, places_ref, count, vecs_ref):
    blocks = vecs_ref.shape[1] - per_piece - 1
    row_base, col_base = lax.axis_index("row") * per_piece, lax.axis_index("col") * per_piece
    i, j = places_ref[0, t], places_ref[1, t]
    diagonal = (i - j == col_base - row_base) & (j >= row_base) & (j < row_base + per_piece)
    source, at, base = (j, i, row_base) if forward else (i, j, col_base)
    source = jnp.where(diagonal, source + (blocks - base), source)
    return jnp.where(t < count, source, blocks + per_piece), at


def forward_kernel(per_piece, list_ref, count_ref, held_ref, *refs):
    *pieces, first_ref, second_ref, vecs_ref, places_ref, list_sem = refs
    list_copy = pltpu.make_async_copy(list_ref, places_ref, list_sem)
    list_copy.start()
    row_at = lax.axis_index("row")
    prepare(turned_vectors, [row_at ^ s for s in range(len(pieces))], pieces, vecs_ref)
    for total_ref in (first_ref, second_ref):
        total_ref[...] = jnp.zeros_like(total_ref)
    list_copy.wait()
    count = count_ref[0, 0]
    side = held_ref.shape[-1]

    @pl.loop(0, (count + GROUP - 1) // GROUP)
    def _(g):
        for u in range(0, GROUP, 2):
            slots = [g * GROUP + u + h for h in range(2)]
            found = [find_slot(True, per_piece, t, places_ref, count, vecs_ref) for t in slots]
            rows = [jnp.concatenate(split(held_ref[t]), axis=1) for t in slots]
            both = vecs_ref[0, found[0][0]] + vecs_ref[1, found[1][0]]
            out = jnp.dot(
                jnp.concatenate(rows, axis=0),
                jnp.concatenate([both, both], axis=0),
                preferred_element_type=jnp.float32,
            )
            for h, total_ref in enumerate((first_ref, second_ref)):
                total_ref[found[h][1]] += out[side * h:side * (h + 1)]


def transposed_kernel(
    per_piece, list_ref, count_ref, held_ref, own_ref, came_ref, _, total_ref, vecs_ref, places_ref, list_sem, *others
):
    list_copy = pltpu.make_async_copy(list_ref, places_ref, list_sem)
    list_copy.start()
    half = own_ref.shape[0]
    origins = [shifted(-2 * q, 2 * half) for q in range(half)]
    prepare(
        plain_vectors,
        origins + [origin ^ 1 for origin in origins],
        [ref.at[q] for ref in (own_ref, came_ref) for q in range(half)],
        vecs_ref,
    )
    totals = [total_ref, *others]
    for ref in totals:
        ref[...] = jnp.zeros_like(ref)
    list_copy.wait()
    count = count_ref[0, 0]
    width, side = total_ref.shape[1:]

    @pl.loop(0, (count + LONG_GROUP - 1) // LONG_GROUP)
    def _(g):
        for u in range(LONG_GROUP):
            t = g * LONG_GROUP + u
            source, at = find_slot(False, per_piece, t, places_ref, count, vecs_ref)
            out = jnp.dot(
                vecs_ref[0, source],
                jnp.concatenate(split(held_ref[t]), axis=1),
                preferred_element_type=jnp.float32,
            )
            totals[u % len(totals)][at] += out[:width, :side] + out[width:, :side] + out[:width, side:]

    for ref in others:
        total_ref[...] += ref[...]


def route_rows_kernel(other, first_ref, second_ref, out_ref):
    n = 2 * out_ref.shape[0]
    per_piece = first_ref.shape[0] // n
    width = out_ref.shape[1]
    side = first_ref.shape[-1]
    column = lax.broadcasted_iota(jnp.int32, (side, side), 1)
    for q in range(n // 2):
        base = (shifted(2 * q, n) ^ other) * per_piece
        for b in range(per_piece):
            turned = jnp.where(column < side // 2, first_ref[base + b], second_ref[base + b]).T
            block = turned[:width]
            for v in range(width, side, width):
                block = block + turned[v:v + width]
            out_ref[q, :, b * side:(b + 1) * side] = block


def route_cols_kernel(total_ref, *outs):
    width, share = outs[0].shape
    side = total_ref.shape[-1]
    for s, out in enumerate(outs):
        base = (lax.axis_index("row") ^ s) * (share // side)
        for b in range(share // side):
            out[:, b * side:(b + 1) * side] = total_ref[base + b]


def add_kernel(kept_ref, came_ref, *outs):
    for q, out in enumerate(outs):
        out[...] = kept_ref[q] + came_ref[q]


def sum_kernel(*refs):
    *ins, basis_ref, residual_ref = refs
    vec = basis_ref.shape[0]
    total = ins[0][...]
    for ref in ins[1:]:
        total = total + ref[...]
    basis_ref[...] = total[:vec]
    residual_ref[...] = total[vec:]


def exchange(x, axis, offset):
    return lax.ppermute(x, axis, [(a, a ^ offset) for a in range(lax.axis_size(axis))])


def shift(x, steps):
    n = lax.axis_size("col")
    return lax.ppermute(x, "col", [(a, (a + steps) % n) for a in range(n)])


def local(ham_tiles, tile_list, tile_count, basis_block, residual_block):
    slots, side = ham_tiles.shape[2], ham_tiles.shape[-1]
    vec, share = basis_block.shape
    width = 2 * vec
    per_piece = share // side
    n_row, n_col = lax.axis_size("row"), lax.axis_size("col")
    row_blocks, col_blocks = n_col * per_piece, n_row * per_piece
    tiles = ham_tiles[0, 0]
    listing = tile_list[0, 0].T
    def cost(part):
        return pl.CostEstimate(
            flops=int(part * slots * 2 * side * side * width * 24),
            bytes_accessed=int(part * slots * side * side * 4),
            transcendentals=0,
        )

    stacked = lax.pad(basis_block, 0.0, ((0, vec, 0), (0, 0, 0))) + lax.pad(
        residual_block, 0.0, ((vec, 0, 0), (0, 0, 0))
    )
    own = pl.pallas_call(
        pass_kernel,
        out_shape=f32(width, share),
        in_specs=[VMEM],
        out_specs=VMEM,
        compiler_params=pltpu.CompilerParams(vmem_limit_bytes=2 * MIB),
        cost_estimate=cost(4.0),
        name="own_share",
    )(stacked)
    col_pieces = [own] + [exchange(own, "row", s) for s in range(1, n_row)]
    line = [own] + [shift(own, s) for s in reversed(range(2, n_col, 2))][::-1]
    params = pltpu.CompilerParams(vmem_limit_bytes=16 * MIB)
    total, second = pl.pallas_call(
        functools.partial(forward_kernel, per_piece),
        out_shape=[f32(row_blocks, side, side)] * 2,
        in_specs=[ANY, SMEM, VMEM] + [VMEM] * n_row,
        out_specs=[VMEM] * 2,
        scratch_shapes=[
            pltpu.VMEM((2, col_blocks + per_piece + 1, side, side), jnp.bfloat16),
            pltpu.SMEM(listing.shape, jnp.int32),
            pltpu.SemaphoreType.DMA(()),
        ],
        compiler_params=params,
        cost_estimate=cost(1.0),
        name="forward_product",
    )(listing, tile_count, tiles, *col_pieces)
    *line, total = lax.optimization_barrier((*line[::-1], total))
    panel = small(gather_kernel, f32(n_col // 2, width, share), "gather_line", *line)
    came = exchange(panel, "col", 1)
    pieces = f32(n_col // 2, width, share)
    leaving = small(functools.partial(route_rows_kernel, 1), pieces, "route_leaving", total, second)
    from_core = exchange(leaving, "col", 1)
    leaving, total = lax.optimization_barrier((leaving, total))
    kept = small(functools.partial(route_rows_kernel, 0), pieces, "route_kept", total, second)
    piece = f32(width, share)
    line = small(add_kernel, [piece] * (n_col // 2), "add_cores", kept, from_core)
    total = pl.pallas_call(
        functools.partial(transposed_kernel, per_piece),
        out_shape=f32(col_blocks, width, side),
        in_specs=[ANY, SMEM, VMEM, VMEM, VMEM, ANY],
        out_specs=VMEM,
        scratch_shapes=[
            pltpu.VMEM((1, row_blocks + per_piece + 1, 2 * width, side), jnp.bfloat16),
            pltpu.SMEM(listing.shape, jnp.int32),
            pltpu.SemaphoreType.DMA(()),
        ]
        + [pltpu.VMEM((col_blocks, width, side), jnp.float32)] * 3,
        compiler_params=params,
        cost_estimate=cost(1.0),
        name="transposed_product",
    )(listing, tile_count, tiles, panel, came, line[0])
    lines = [line[0]] + [shift(line[q], 2 * q) for q in range(1, n_col // 2)]
    *lines, total = lax.optimization_barrier((*lines, total))
    away = small(route_cols_kernel, [piece] * n_row, "route_columns", total)
    cols = [away[0]] + [exchange(away[s], "row", s) for s in reversed(range(1, n_row))]
    h_basis, h_residual = small(sum_kernel, [f32(vec, share)] * 2, "sum_pieces", *lines, *cols)
    return (h_basis, h_residual)


def solution(mesh):
    placed = (
        P("row", "col", None, None, None),
        P("row", "col", None, None),
        P("row", "col"),
        P(None, ("row", "col")),
        P(None, ("row", "col")),
    )
    return jax.shard_map(
        local,
        mesh=mesh,
        in_specs=placed,
        out_specs=(P(None, ("row", "col")), P(None, ("row", "col"))),
        check_vma=False,
    )
```

profile of v0, /device:TPU:0, one launch (start us, length us, event | category | flops | bytes accessed | tf_op | source)
XLA Modules:
  0.0 37.1 jit_solution(4709822447596729328)
XLA Ops:
  0.6 0.8 %pad_add_fusion.in_ref = f32[32,512]{1,0:T(8,128)S(1)} fusion(f32[16,512]{1,0:T(8,128)} %param.9, f32[16,512]{1,0:T(8,128)} %param.8), kind=kLoop, calls=%fused_computation | loop fusion | flops 16384 | bytes 131072 | tf_op jit(solution)/shard_map/add | solution.py:221
  1.4 0.0 copy-start
  1.4 0.0 copy-start.1
  1.4 4.0 %collective-permute-start.5 = (f32[32,512]{1,0:T(8,128)S(1)}, f32[32,512]{1,0:T(8,128)S(1)}, u32[]{:S(2)}, u32[]{:S(2)}) collective-permute-start(f32[32,512]{1,0:T(8,128)S(1)} %own_share.1.refs_0_.refs_3_), channel_id=1, source_target_pairs={{0,24},{8,16},{16,8},{24,0},{1,25},{9,17},{17,9},{25,1},{2,26},{10... | collective-permute-start | bytes 196616 | tf_op jit(solution)/shard_map/ppermute | solution.py:197
  5.4 0.5 %collective-permute-start.4 = (f32[32,512]{1,0:T(8,128)S(1)}, f32[32,512]{1,0:T(8,128)S(1)}, u32[]{:S(2)}, u32[]{:S(2)}) collective-permute-start(f32[32,512]{1,0:T(8,128)S(1)} %own_share.1.refs_0_.refs_3_), channel_id=1, source_target_pairs={{0,16},{8,24},{16,0},{24,8},{1,17},{9,25},{17,1},{25,9},{2,18},{10... | collective-permute-start | bytes 196616 | tf_op jit(solution)/shard_map/ppermute | solution.py:197
  5.9 0.1 collective-permute-start.3
  6.0 2.0 %collective-permute-start.2 = (f32[32,512]{1,0:T(8,128)S(1)}, f32[32,512]{1,0:T(8,128)S(1)}, u32[]{:S(2)}, u32[]{:S(2)}) collective-permute-start(f32[32,512]{1,0:T(8,128)S(1)} %own_share.1.refs_0_.refs_3_), channel_id=1, source_target_pairs={{0,2},{1,3},{2,4},{3,5},{4,6},{5,7},{6,0},{7,1},{8,10},{9,11},{10,... | collective-permute-start | bytes 196616 | tf_op jit(solution)/shard_map/ppermute | solution.py:202
  8.0 2.6 %collective-permute-start.1 = (f32[32,512]{1,0:T(8,128)S(1)}, f32[32,512]{1,0:T(8,128)S(1)}, u32[]{:S(2)}, u32[]{:S(2)}) collective-permute-start(f32[32,512]{1,0:T(8,128)S(1)} %own_share.1.refs_0_.refs_3_), channel_id=1, source_target_pairs={{0,4},{1,5},{2,6},{3,7},{4,0},{5,1},{6,2},{7,3},{8,12},{9,13},{10,... | collective-permute-start | bytes 196616 | tf_op jit(solution)/shard_map/ppermute | solution.py:202
  11.3 0.0 collective-permute-done.5.refs_3_
  11.3 1.9 %collective-permute-start = (f32[32,512]{1,0:T(8,128)S(1)}, f32[32,512]{1,0:T(8,128)S(1)}, u32[]{:S(2)}, u32[]{:S(2)}) collective-permute-start(f32[32,512]{1,0:T(8,128)S(1)} %own_share.1.refs_0_.refs_3_), channel_id=1, source_target_pairs={{0,6},{1,7},{2,0},{3,1},{4,2},{5,3},{6,4},{7,5},{8,14},{9,15},{10,... | collective-permute-start | bytes 196616 | tf_op jit(solution)/shard_map/ppermute | solution.py:202
  13.2 0.0 collective-permute-done.4.refs_2_
  13.2 0.0 collective-permute-done.3.refs_1_
  13.2 0.0 copy-done
  13.2 0.0 copy-done.1
  13.2 6.7 %forward_product.1 = (f32[32,128,128]{2,1,0:T(8,128)S(1)}, f32[32,128,128]{2,1,0:T(8,128)S(1)}) custom-call(s32[2,320]{1,0:T(2,128)S(1)} %bitcast.6, s32[1,1]{1,0:T(1,128)S(6)} %copy.7.count_ref, f32[320,128,128]{2,1,0:T(8,128)S(1)} %bitcast.4, f32[32,512]{1,0:T(8,128)S(1)} %own_share.1.refs_0_.refs_3_, f32[32,512]{1,0:T(8,128)S(1)} %collective-permute-done.3.refs_1_, ...), custom_call_target="tpu_custom_call" | custom-call | flops 8053063680 | bytes 20971520 | tf_op jit(solution)/shard_map/forward_product/pallas_call | solution.py:236
  19.9 0.0 collective-permute-done.2.refs_2_
  19.9 0.0 collective-permute-done.1.refs_1_
  19.9 0.0 collective-permute-done.refs_0_
  19.9 0.3 route_leaving.1
  20.3 0.1 collective-permute-start.6
  20.4 0.6 %collective-permute-start.10 = (f32[4,32,512]{2,1,0:T(8,128)S(1)}, f32[4,32,512]{2,1,0:T(8,128)S(1)}, u32[]{:S(2)}, u32[]{:S(2)}) collective-permute-start(f32[4,32,512]{2,1,0:T(8,128)S(1)} %gather_line.1.own_ref), channel_id=1, source_target_pairs={{0,1},{1,0},{2,3},{3,2},{4,5},{5,4},{6,7},{7,6},{8,9},{9,8},{10,11... | collective-permute-start | bytes 786440 | tf_op jit(solution)/shard_map/ppermute | solution.py:197
  20.9 0.3 route_kept.1.kept_ref
  21.3 0.6 %collective-permute-done.6.came_ref = f32[4,32,512]{2,1,0:T(8,128)S(1)} collective-permute-done((f32[4,32,512]{2,1,0:T(8,128)S(1)}, f32[4,32,512]{2,1,0:T(8,128)S(1)}, u32[]{:S(2)}, u32[]{:S(2)}) %collective-permute-start.6) | collective-permute-done | bytes 262176 | tf_op jit(solution)/shard_map/ppermute | solution.py:197
  21.9 0.1 collective-permute-start.7
  22.0 1.8 %collective-permute-start.8 = (f32[32,512]{1,0:T(8,128)S(1)}, f32[32,512]{1,0:T(8,128)S(1)}, u32[]{:S(2)}, u32[]{:S(2)}) collective-permute-start(f32[32,512]{1,0:T(8,128)S(1)} %get-tuple-element.29), channel_id=1, source_target_pairs={{0,4},{1,5},{2,6},{3,7},{4,0},{5,1},{6,2},{7,3},{8,12},{9,13},{10,... | collective-permute-start | bytes 196616 | tf_op jit(solution)/shard_map/ppermute | solution.py:202
  23.8 2.0 %collective-permute-start.9 = (f32[32,512]{1,0:T(8,128)S(1)}, f32[32,512]{1,0:T(8,128)S(1)}, u32[]{:S(2)}, u32[]{:S(2)}) collective-permute-start(f32[32,512]{1,0:T(8,128)S(1)} %get-tuple-element.30), channel_id=1, source_target_pairs={{0,6},{1,7},{2,0},{3,1},{4,2},{5,3},{6,4},{7,5},{8,14},{9,15},{10,... | collective-permute-start | bytes 196616 | tf_op jit(solution)/shard_map/ppermute | solution.py:202
  25.8 0.0 collective-permute-done.10.came_ref
  25.8 3.7 %transposed_product.1.total_ref = f32[16,32,128]{2,1,0:T(8,128)S(1)} custom-call(s32[2,320]{1,0:T(2,128)S(1)} %bitcast.7, s32[1,1]{1,0:T(1,128)S(6)} %copy.7.count_ref, f32[320,128,128]{2,1,0:T(8,128)S(1)} %bitcast.5, f32[4,32,512]{2,1,0:T(8,128)S(1)} %gather_line.1.own_ref, f32[4,32,512]{2,1,0:T(8,128)S(1)} %collective-permute-done.10.came_ref, ...), custom_call_target="tpu_custom_call" | custom-call | flops 8053063680 | bytes 20971520 | tf_op jit(solution)/shard_map/transposed_product/pallas_call | solution.py:260
  29.5 0.0 collective-permute-done.7.refs_1_
  29.5 1.1 %collective-permute-done.8.refs_2_ = f32[32,512]{1,0:T(8,128)S(1)} collective-permute-done((f32[32,512]{1,0:T(8,128)S(1)}, f32[32,512]{1,0:T(8,128)S(1)}, u32[]{:S(2)}, u32[]{:S(2)}) %collective-permute-start.8) | collective-permute-done | bytes 65568 | tf_op jit(solution)/shard_map/ppermute | solution.py:202
  30.6 0.0 collective-permute-done.9.refs_3_
  30.6 0.1 collective-permute-start.11
  30.7 0.2 collective-permute-start.12
  30.9 3.3 %collective-permute-start.13 = (f32[32,512]{1,0:T(8,128)S(1)}, f32[32,512]{1,0:T(8,128)S(1)}, u32[]{:S(2)}, u32[]{:S(2)}) collective-permute-start(f32[32,512]{1,0:T(8,128)S(1)} %get-tuple-element.43), channel_id=1, source_target_pairs={{0,8},{8,0},{16,24},{24,16},{1,9},{9,1},{17,25},{25,17},{2,10},{10... | collective-permute-start | bytes 196616 | tf_op jit(solution)/shard_map/ppermute | solution.py:197
  34.2 1.7 %collective-permute-done.11.refs_5_ = f32[32,512]{1,0:T(8,128)S(1)} collective-permute-done((f32[32,512]{1,0:T(8,128)S(1)}, f32[32,512]{1,0:T(8,128)S(1)}, u32[]{:S(2)}, u32[]{:S(2)}) %collective-permute-start.11) | collective-permute-done | bytes 65568 | tf_op jit(solution)/shard_map/ppermute | solution.py:197
  35.9 0.0 collective-permute-done.12.refs_6_
  35.9 0.6 %collective-permute-done.13.refs_7_ = f32[32,512]{1,0:T(8,128)S(1)} collective-permute-done((f32[32,512]{1,0:T(8,128)S(1)}, f32[32,512]{1,0:T(8,128)S(1)}, u32[]{:S(2)}, u32[]{:S(2)}) %collective-permute-start.13) | collective-permute-done | bytes 65568 | tf_op jit(solution)/shard_map/ppermute | solution.py:197
  36.4 0.6 %sum_pieces.1 = (f32[16,512]{1,0:T(8,128)}, f32[16,512]{1,0:T(8,128)}) custom-call(f32[32,512]{1,0:T(8,128)S(1)} %get-tuple-element.35._.refs_0_, f32[32,512]{1,0:T(8,128)S(1)} %collective-permute-done.7.refs_1_, f32[32,512]{1,0:T(8,128)S(1)} %collective-permute-done.8.refs_2_, f32[32,512]{1,0:T(8,128)S(1)} %collective-permute-done.9.refs_3_, ...), custom_call_target="tpu_custom_call" | custom-call | tf_op jit(solution)/shard_map/sum_pieces/pallas_call | solution.py:20
  (4 shorter events, 0.1 us)
Async XLA Ops:
  1.4 11.8 %copy-start = (f32[1,1,320,128,128]{4,3,2,1,0:T(8,128)S(1)}, f32[1,1,320,128,128]{4,3,2,1,0:T(8,128)}, u32[]{:S(2)}) copy-start(f32[1,1,320,128,128]{4,3,2,1,0:T(8,128)} %param.5) | copy-start | bytes 62914564
  1.4 11.8 %copy-start.1 = (s32[1,1,320,2]{2,3,1,0:T(2,128)S(1)}, s32[1,1,320,2]{2,3,1,0:T(2,128)}, u32[]{:S(2)}) copy-start(s32[1,1,320,2]{2,3,1,0:T(2,128)} %param.6) | copy-start | bytes 7684
  1.4 9.8 %collective-permute-start.5 = (f32[32,512]{1,0:T(8,128)S(1)}, f32[32,512]{1,0:T(8,128)S(1)}, u32[]{:S(2)}, u32[]{:S(2)}) collective-permute-start(f32[32,512]{1,0:T(8,128)S(1)} %own_share.1.refs_0_.refs_3_), channel_id=1, source_target_pairs={{0,24},{8,16},{16,8},{24,0},{1,25},{9,17},{17,9},{25,1},{2,26},{10... | collective-permute-start | bytes 196616 | tf_op jit(solution)/shard_map/ppermute | solution.py:197
  5.4 7.8 %collective-permute-start.4 = (f32[32,512]{1,0:T(8,128)S(1)}, f32[32,512]{1,0:T(8,128)S(1)}, u32[]{:S(2)}, u32[]{:S(2)}) collective-permute-start(f32[32,512]{1,0:T(8,128)S(1)} %own_share.1.refs_0_.refs_3_), channel_id=1, source_target_pairs={{0,16},{8,24},{16,0},{24,8},{1,17},{9,25},{17,1},{25,9},{2,18},{10... | collective-permute-start | bytes 196616 | tf_op jit(solution)/shard_map/ppermute | solution.py:197
  5.9 7.3 %collective-permute-start.3 = (f32[32,512]{1,0:T(8,128)S(1)}, f32[32,512]{1,0:T(8,128)S(1)}, u32[]{:S(2)}, u32[]{:S(2)}) collective-permute-start(f32[32,512]{1,0:T(8,128)S(1)} %own_share.1.refs_0_.refs_3_), channel_id=1, source_target_pairs={{0,8},{8,0},{16,24},{24,16},{1,9},{9,1},{17,25},{25,17},{2,10},{10... | collective-permute-start | bytes 196616 | tf_op jit(solution)/shard_map/ppermute | solution.py:197
  6.0 13.9 %collective-permute-start.2 = (f32[32,512]{1,0:T(8,128)S(1)}, f32[32,512]{1,0:T(8,128)S(1)}, u32[]{:S(2)}, u32[]{:S(2)}) collective-permute-start(f32[32,512]{1,0:T(8,128)S(1)} %own_share.1.refs_0_.refs_3_), channel_id=1, source_target_pairs={{0,2},{1,3},{2,4},{3,5},{4,6},{5,7},{6,0},{7,1},{8,10},{9,11},{10,... | collective-permute-start | bytes 196616 | tf_op jit(solution)/shard_map/ppermute | solution.py:202
  8.0 11.9 %collective-permute-start.1 = (f32[32,512]{1,0:T(8,128)S(1)}, f32[32,512]{1,0:T(8,128)S(1)}, u32[]{:S(2)}, u32[]{:S(2)}) collective-permute-start(f32[32,512]{1,0:T(8,128)S(1)} %own_share.1.refs_0_.refs_3_), channel_id=1, source_target_pairs={{0,4},{1,5},{2,6},{3,7},{4,0},{5,1},{6,2},{7,3},{8,12},{9,13},{10,... | collective-permute-start | bytes 196616 | tf_op jit(solution)/shard_map/ppermute | solution.py:202
  11.3 8.7 %collective-permute-start = (f32[32,512]{1,0:T(8,128)S(1)}, f32[32,512]{1,0:T(8,128)S(1)}, u32[]{:S(2)}, u32[]{:S(2)}) collective-permute-start(f32[32,512]{1,0:T(8,128)S(1)} %own_share.1.refs_0_.refs_3_), channel_id=1, source_target_pairs={{0,6},{1,7},{2,0},{3,1},{4,2},{5,3},{6,4},{7,5},{8,14},{9,15},{10,... | collective-permute-start | bytes 196616 | tf_op jit(solution)/shard_map/ppermute | solution.py:202
  20.3 1.6 %collective-permute-start.6 = (f32[4,32,512]{2,1,0:T(8,128)S(1)}, f32[4,32,512]{2,1,0:T(8,128)S(1)}, u32[]{:S(2)}, u32[]{:S(2)}) collective-permute-start(f32[4,32,512]{2,1,0:T(8,128)S(1)} %route_leaving.1), channel_id=1, source_target_pairs={{0,1},{1,0},{2,3},{3,2},{4,5},{5,4},{6,7},{7,6},{8,9},{9,8},{10,11... | collective-permute-start | bytes 786440 | tf_op jit(solution)/shard_map/ppermute | solution.py:197
  20.4 5.4 %collective-permute-start.10 = (f32[4,32,512]{2,1,0:T(8,128)S(1)}, f32[4,32,512]{2,1,0:T(8,128)S(1)}, u32[]{:S(2)}, u32[]{:S(2)}) collective-permute-start(f32[4,32,512]{2,1,0:T(8,128)S(1)} %gather_line.1.own_ref), channel_id=1, source_target_pairs={{0,1},{1,0},{2,3},{3,2},{4,5},{5,4},{6,7},{7,6},{8,9},{9,8},{10,11... | collective-permute-start | bytes 786440 | tf_op jit(solution)/shard_map/ppermute | solution.py:197
  21.9 7.6 %collective-permute-start.7 = (f32[32,512]{1,0:T(8,128)S(1)}, f32[32,512]{1,0:T(8,128)S(1)}, u32[]{:S(2)}, u32[]{:S(2)}) collective-permute-start(f32[32,512]{1,0:T(8,128)S(1)} %get-tuple-element.28), channel_id=1, source_target_pairs={{0,2},{1,3},{2,4},{3,5},{4,6},{5,7},{6,0},{7,1},{8,10},{9,11},{10,... | collective-permute-start | bytes 196616 | tf_op jit(solution)/shard_map/ppermute | solution.py:202
  22.0 8.6 %collective-permute-start.8 = (f32[32,512]{1,0:T(8,128)S(1)}, f32[32,512]{1,0:T(8,128)S(1)}, u32[]{:S(2)}, u32[]{:S(2)}) collective-permute-start(f32[32,512]{1,0:T(8,128)S(1)} %get-tuple-element.29), channel_id=1, source_target_pairs={{0,4},{1,5},{2,6},{3,7},{4,0},{5,1},{6,2},{7,3},{8,12},{9,13},{10,... | collective-permute-start | bytes 196616 | tf_op jit(solution)/shard_map/ppermute | solution.py:202
  23.8 6.8 %collective-permute-start.9 = (f32[32,512]{1,0:T(8,128)S(1)}, f32[32,512]{1,0:T(8,128)S(1)}, u32[]{:S(2)}, u32[]{:S(2)}) collective-permute-start(f32[32,512]{1,0:T(8,128)S(1)} %get-tuple-element.30), channel_id=1, source_target_pairs={{0,6},{1,7},{2,0},{3,1},{4,2},{5,3},{6,4},{7,5},{8,14},{9,15},{10,... | collective-permute-start | bytes 196616 | tf_op jit(solution)/shard_map/ppermute | solution.py:202
  30.6 5.2 %collective-permute-start.11 = (f32[32,512]{1,0:T(8,128)S(1)}, f32[32,512]{1,0:T(8,128)S(1)}, u32[]{:S(2)}, u32[]{:S(2)}) collective-permute-start(f32[32,512]{1,0:T(8,128)S(1)} %get-tuple-element.41), channel_id=1, source_target_pairs={{0,24},{8,16},{16,8},{24,0},{1,25},{9,17},{17,9},{25,1},{2,26},{10... | collective-permute-start | bytes 196616 | tf_op jit(solution)/shard_map/ppermute | solution.py:197
  30.7 5.2 %collective-permute-start.12 = (f32[32,512]{1,0:T(8,128)S(1)}, f32[32,512]{1,0:T(8,128)S(1)}, u32[]{:S(2)}, u32[]{:S(2)}) collective-permute-start(f32[32,512]{1,0:T(8,128)S(1)} %get-tuple-element.42), channel_id=1, source_target_pairs={{0,16},{8,24},{16,0},{24,8},{1,17},{9,25},{17,1},{25,9},{2,18},{10... | collective-permute-start | bytes 196616 | tf_op jit(solution)/shard_map/ppermute | solution.py:197
  30.9 5.6 %collective-permute-start.13 = (f32[32,512]{1,0:T(8,128)S(1)}, f32[32,512]{1,0:T(8,128)S(1)}, u32[]{:S(2)}, u32[]{:S(2)}) collective-permute-start(f32[32,512]{1,0:T(8,128)S(1)} %get-tuple-element.43), channel_id=1, source_target_pairs={{0,8},{8,0},{16,24},{24,16},{1,9},{9,1},{17,25},{25,17},{2,10},{10... | collective-permute-start | bytes 196616 | tf_op jit(solution)/shard_map/ppermute | solution.py:197
where the time goes:
time: 37 us; the launch traced here: 37.1 us
  starting transfers between devices  19.1 us (52%)
  Pallas kernels  11.8 us (32%)
  waiting for transfers between devices  3.94 us (11%)
  between operations  1.43 us (4%)
  other arithmetic  0.78 us (2%)
    ppermute x6, starting transfers between devices, shift(): return lax.ppermute(x, 'col', [(a, (a + steps) % n) for a in range(n)])  10.3 us
    ppermute x8, starting transfers between devices, exchange(): lax.ppermute(x, axis, [(a, a ^ offset) for a in range(lax.axis_size(axis))])  8.77 us
    pallas_call x1, Pallas kernels, local(): pl.pallas_call(functools.partial(forward_kernel, per_piece), out_shape=[f...  6.71 us
    pallas_call x1, Pallas kernels, local(): pl.pallas_call(functools.partial(transposed_kernel, per_piece), out_shape...  3.71 us
    ppermute x8, waiting for transfers between devices, exchange(): lax.ppermute(x, axis, [(a, a ^ offset) for a in range(lax.axis_size(axis))])  2.84 us
    pallas_call x6, Pallas kernels, small(): pl.pallas_call(kernel, out_shape=out_shape, in_specs=in_specs or [VMEM] *...  1.4 us
    ppermute x6, waiting for transfers between devices, shift(): return lax.ppermute(x, 'col', [(a, (a + steps) % n) for a in range(n)])  1.1 us
    add x1, other arithmetic, local(): lax.pad(basis_block, 0.0, ((0, vec, 0), (0, 0, 0)))  0.78 us
  transfers between devices with their start and end apart: 14, of which 4 were waited for; matrix products, arithmetic and copies ran while one was open for 0% of the time, Pallas kernels for 29%

commit v1 on v0

--- a/solution.py
+++ b/solution.py
@@ -7,8 +7,8 @@
 from jax.experimental.pallas import tpu as pltpu
 from jax.sharding import PartitionSpec as P
 
-GROUP = 32
-LONG_GROUP = 64
+FORWARD_GROUP = 64
+TRANSPOSED_GROUP = 160
 MIB = 1024 * 1024
 VMEM = pl.BlockSpec(memory_space=pltpu.VMEM)
 SMEM = pl.BlockSpec(memory_space=pltpu.SMEM)
@@ -101,10 +101,10 @@
     count = count_ref[0, 0]
     side = held_ref.shape[-1]
 
-    @pl.loop(0, (count + GROUP - 1) // GROUP)
+    @pl.loop(0, (count + FORWARD_GROUP - 1) // FORWARD_GROUP)
     def _(g):
-        for u in range(0, GROUP, 2):
-            slots = [g * GROUP + u + h for h in range(2)]
+        for u in range(0, FORWARD_GROUP, 2):
+            slots = [g * FORWARD_GROUP + u + h for h in range(2)]
             found = [find_slot(True, per_piece, t, places_ref, count, vecs_ref) for t in slots]
             rows = [jnp.concatenate(split(held_ref[t]), axis=1) for t in slots]
             both = vecs_ref[0, found[0][0]] + vecs_ref[1, found[1][0]]
@@ -137,10 +137,10 @@
     count = count_ref[0, 0]
     width, side = total_ref.shape[1:]
 
-    @pl.loop(0, (count + LONG_GROUP - 1) // LONG_GROUP)
+    @pl.loop(0, (count + TRANSPOSED_GROUP - 1) // TRANSPOSED_GROUP)
     def _(g):
-        for u in range(LONG_GROUP):
-            t = g * LONG_GROUP + u
+        for u in range(TRANSPOSED_GROUP):
+            t = g * TRANSPOSED_GROUP + u
             source, at = find_slot(False, per_piece, t, places_ref, count, vecs_ref)
             out = jnp.dot(
                 vecs_ref[0, source],
@@ -181,6 +181,14 @@
 def add_kernel(kept_ref, came_ref, *outs):
     for q, out in enumerate(outs):
         out[...] = kept_ref[q] + came_ref[q]
+
+
+def line_kernel(*refs):
+    *ins, out_ref = refs
+    total = ins[0][...]
+    for ref in ins[1:]:
+        total = total + ref[...]
+    out_ref[...] = total
 
 
 def sum_kernel(*refs):
@@ -273,10 +281,10 @@
         name="transposed_product",
     )(listing, tile_count, tiles, panel, came, line[0])
     lines = [line[0]] + [shift(line[q], 2 * q) for q in range(1, n_col // 2)]
-    *lines, total = lax.optimization_barrier((*lines, total))
     away = small(route_cols_kernel, [piece] * n_row, "route_columns", total)
-    cols = [away[0]] + [exchange(away[s], "row", s) for s in reversed(range(1, n_row))]
-    h_basis, h_residual = small(sum_kernel, [f32(vec, share)] * 2, "sum_pieces", *lines, *cols)
+    cols = [exchange(away[s], "row", s) for s in reversed(range(1, n_row))]
+    along = small(line_kernel, piece, "sum_line", *lines, away[0])
+    h_basis, h_residual = small(sum_kernel, [f32(vec, share)] * 2, "sum_pieces", along, *cols)
     return (h_basis, h_residual)
 
 

time: 37 us -> 34.8 us (0.941); the launches traced: 37.1 us -> 34.5 us
  Pallas kernels: 11.8 us -> 8.52 us
  waiting for transfers between devices: 3.94 us -> 4.46 us
    pallas_call x1, Pallas kernels: 6.71 us -> 4.73 us  [local(): pl.pallas_call(functools.partial(forward_kernel, per_piece), out_shape=[f...]
    ppermute x8, waiting for transfers between devices: 2.84 us -> 4.45 us  [exchange(): lax.ppermute(x, axis, [(a, a ^ offset) for a in range(lax.axis_size(axis))])]
    pallas_call x1, Pallas kernels: 3.71 us -> 2.36 us  [local(): pl.pallas_call(functools.partial(transposed_kernel, per_piece), out_shape...]
    ppermute x6, waiting for transfers between devices: 1.1 us -> 0.02 us  [shift(): return lax.ppermute(x, 'col', [(a, (a + steps) % n) for a in range(n)])]
    pallas_call x6 -> x7, Pallas kernels: 1.4 us -> 1.42 us  [small(): pl.pallas_call(kernel, out_shape=out_shape, in_specs=in_specs or [VMEM] *...]
  transfers between devices with their start and end apart: 14 -> 14, of which waited for: 4 -> 4; matrix products, arithmetic and copies ran while one was open for 0% -> 0% of each run, Pallas kernels for 29% -> 22%
where the time goes in v1:
time: 34.8 us; the launch traced here: 34.5 us
  starting transfers between devices  19.3 us (55%)
  Pallas kernels  8.52 us (24%)
  waiting for transfers between devices  4.46 us (13%)
  between operations  1.41 us (4%)
  other arithmetic  0.78 us (2%)
    ppermute x6, starting transfers between devices, shift(): return lax.ppermute(x, 'col', [(a, (a + steps) % n) for a in range(n)])  10.5 us
    ppermute x8, starting transfers between devices, exchange(): lax.ppermute(x, axis, [(a, a ^ offset) for a in range(lax.axis_size(axis))])  8.78 us
    pallas_call x1, Pallas kernels, local(): pl.pallas_call(functools.partial(forward_kernel, per_piece), out_shape=[f...  4.73 us
    ppermute x8, waiting for transfers between devices, exchange(): lax.ppermute(x, axis, [(a, a ^ offset) for a in range(lax.axis_size(axis))])  4.45 us
    pallas_call x1, Pallas kernels, local(): pl.pallas_call(functools.partial(transposed_kernel, per_piece), out_shape...  2.36 us
    pallas_call x7, Pallas kernels, small(): pl.pallas_call(kernel, out_shape=out_shape, in_specs=in_specs or [VMEM] *...  1.42 us
    add x1, other arithmetic, local(): lax.pad(basis_block, 0.0, ((0, vec, 0), (0, 0, 0)))  0.78 us
  transfers between devices with their start and end apart: 14, of which 4 were waited for; matrix products, arithmetic and copies ran while one was open for 0% of the time, Pallas kernels for 22%

profile of v1, /device:TPU:0, one launch (start us, length us, event | category | flops | bytes accessed | tf_op | source)
XLA Modules:
  0.0 34.5 jit_solution(14557519019474080573)
XLA Ops:
  0.6 0.8 %pad_add_fusion.in_ref = f32[32,512]{1,0:T(8,128)S(1)} fusion(f32[16,512]{1,0:T(8,128)} %param.9, f32[16,512]{1,0:T(8,128)} %param.8), kind=kLoop, calls=%fused_computation | loop fusion | flops 16384 | bytes 131072 | tf_op jit(solution)/shard_map/add | solution.py:229
  1.4 0.0 copy-start
  1.4 0.0 copy-start.1
  1.4 4.0 %collective-permute-start.5 = (f32[32,512]{1,0:T(8,128)S(1)}, f32[32,512]{1,0:T(8,128)S(1)}, u32[]{:S(2)}, u32[]{:S(2)}) collective-permute-start(f32[32,512]{1,0:T(8,128)S(1)} %own_share.1.refs_0_.refs_3_), channel_id=1, source_target_pairs={{0,24},{8,16},{16,8},{24,0},{1,25},{9,17},{17,9},{25,1},{2,26},{10... | collective-permute-start | bytes 196616 | tf_op jit(solution)/shard_map/ppermute | solution.py:205
  5.4 0.5 %collective-permute-start.4 = (f32[32,512]{1,0:T(8,128)S(1)}, f32[32,512]{1,0:T(8,128)S(1)}, u32[]{:S(2)}, u32[]{:S(2)}) collective-permute-start(f32[32,512]{1,0:T(8,128)S(1)} %own_share.1.refs_0_.refs_3_), channel_id=1, source_target_pairs={{0,16},{8,24},{16,0},{24,8},{1,17},{9,25},{17,1},{25,9},{2,18},{10... | collective-permute-start | bytes 196616 | tf_op jit(solution)/shard_map/ppermute | solution.py:205
  5.9 0.1 collective-permute-start.3
  6.0 2.0 %collective-permute-start.2 = (f32[32,512]{1,0:T(8,128)S(1)}, f32[32,512]{1,0:T(8,128)S(1)}, u32[]{:S(2)}, u32[]{:S(2)}) collective-permute-start(f32[32,512]{1,0:T(8,128)S(1)} %own_share.1.refs_0_.refs_3_), channel_id=1, source_target_pairs={{0,2},{1,3},{2,4},{3,5},{4,6},{5,7},{6,0},{7,1},{8,10},{9,11},{10,... | collective-permute-start | bytes 196616 | tf_op jit(solution)/shard_map/ppermute | solution.py:210
  8.0 2.6 %collective-permute-start.1 = (f32[32,512]{1,0:T(8,128)S(1)}, f32[32,512]{1,0:T(8,128)S(1)}, u32[]{:S(2)}, u32[]{:S(2)}) collective-permute-start(f32[32,512]{1,0:T(8,128)S(1)} %own_share.1.refs_0_.refs_3_), channel_id=1, source_target_pairs={{0,4},{1,5},{2,6},{3,7},{4,0},{5,1},{6,2},{7,3},{8,12},{9,13},{10,... | collective-permute-start | bytes 196616 | tf_op jit(solution)/shard_map/ppermute | solution.py:210
  11.3 0.0 collective-permute-done.5.refs_3_
  11.3 1.9 %collective-permute-start = (f32[32,512]{1,0:T(8,128)S(1)}, f32[32,512]{1,0:T(8,128)S(1)}, u32[]{:S(2)}, u32[]{:S(2)}) collective-permute-start(f32[32,512]{1,0:T(8,128)S(1)} %own_share.1.refs_0_.refs_3_), channel_id=1, source_target_pairs={{0,6},{1,7},{2,0},{3,1},{4,2},{5,3},{6,4},{7,5},{8,14},{9,15},{10,... | collective-permute-start | bytes 196616 | tf_op jit(solution)/shard_map/ppermute | solution.py:210
  13.2 0.0 collective-permute-done.4.refs_2_
  13.2 0.0 collective-permute-done.3.refs_1_
  13.2 0.0 copy-done
  13.2 0.0 copy-done.1
  13.2 4.7 %forward_product.1 = (f32[32,128,128]{2,1,0:T(8,128)S(1)}, f32[32,128,128]{2,1,0:T(8,128)S(1)}) custom-call(s32[2,320]{1,0:T(2,128)S(1)} %bitcast.6, s32[1,1]{1,0:T(1,128)S(6)} %copy.7.count_ref, f32[320,128,128]{2,1,0:T(8,128)S(1)} %bitcast.4, f32[32,512]{1,0:T(8,128)S(1)} %own_share.1.refs_0_.refs_3_, f32[32,512]{1,0:T(8,128)S(1)} %collective-permute-done.3.refs_1_, ...), custom_call_target="tpu_custom_call" | custom-call | flops 8053063680 | bytes 20971520 | tf_op jit(solution)/shard_map/forward_product/pallas_call | solution.py:244
  17.9 0.0 collective-permute-done.2.refs_2_
  17.9 0.0 collective-permute-done.1.refs_1_
  17.9 0.0 collective-permute-done.refs_0_
  17.9 0.3 %route_leaving.1 = f32[4,32,512]{2,1,0:T(8,128)S(1)} custom-call(f32[32,128,128]{2,1,0:T(8,128)S(1)} %get-tuple-element.21.first_ref, f32[32,128,128]{2,1,0:T(8,128)S(1)} %get-tuple-element.20.second_ref), custom_call_target="tpu_custom_call" | custom-call | tf_op jit(solution)/shard_map/route_leaving/pallas_call | solution.py:20
  18.3 0.1 collective-permute-start.6
  18.4 0.6 %collective-permute-start.10 = (f32[4,32,512]{2,1,0:T(8,128)S(1)}, f32[4,32,512]{2,1,0:T(8,128)S(1)}, u32[]{:S(2)}, u32[]{:S(2)}) collective-permute-start(f32[4,32,512]{2,1,0:T(8,128)S(1)} %gather_line.1.own_ref), channel_id=1, source_target_pairs={{0,1},{1,0},{2,3},{3,2},{4,5},{5,4},{6,7},{7,6},{8,9},{9,8},{10,11... | collective-permute-start | bytes 786440 | tf_op jit(solution)/shard_map/ppermute | solution.py:205
  19.0 0.3 route_kept.1.kept_ref
  19.3 0.6 %collective-permute-done.6.came_ref = f32[4,32,512]{2,1,0:T(8,128)S(1)} collective-permute-done((f32[4,32,512]{2,1,0:T(8,128)S(1)}, f32[4,32,512]{2,1,0:T(8,128)S(1)}, u32[]{:S(2)}, u32[]{:S(2)}) %collective-permute-start.6) | collective-permute-done | bytes 262176 | tf_op jit(solution)/shard_map/ppermute | solution.py:205
  19.9 1.6 %collective-permute-start.7 = (f32[32,512]{1,0:T(8,128)S(1)}, f32[32,512]{1,0:T(8,128)S(1)}, u32[]{:S(2)}, u32[]{:S(2)}) collective-permute-start(f32[32,512]{1,0:T(8,128)S(1)} %get-tuple-element.23), channel_id=1, source_target_pairs={{0,2},{1,3},{2,4},{3,5},{4,6},{5,7},{6,0},{7,1},{8,10},{9,11},{10,... | collective-permute-start | bytes 196616 | tf_op jit(solution)/shard_map/ppermute | solution.py:210
  21.5 1.5 %collective-permute-start.8 = (f32[32,512]{1,0:T(8,128)S(1)}, f32[32,512]{1,0:T(8,128)S(1)}, u32[]{:S(2)}, u32[]{:S(2)}) collective-permute-start(f32[32,512]{1,0:T(8,128)S(1)} %get-tuple-element.24), channel_id=1, source_target_pairs={{0,4},{1,5},{2,6},{3,7},{4,0},{5,1},{6,2},{7,3},{8,12},{9,13},{10,... | collective-permute-start | bytes 196616 | tf_op jit(solution)/shard_map/ppermute | solution.py:210
  23.0 1.0 %collective-permute-start.9 = (f32[32,512]{1,0:T(8,128)S(1)}, f32[32,512]{1,0:T(8,128)S(1)}, u32[]{:S(2)}, u32[]{:S(2)}) collective-permute-start(f32[32,512]{1,0:T(8,128)S(1)} %get-tuple-element.25), channel_id=1, source_target_pairs={{0,6},{1,7},{2,0},{3,1},{4,2},{5,3},{6,4},{7,5},{8,14},{9,15},{10,... | collective-permute-start | bytes 196616 | tf_op jit(solution)/shard_map/ppermute | solution.py:210
  24.0 0.0 collective-permute-done.10.came_ref
  24.0 2.4 %transposed_product.1.total_ref = f32[16,32,128]{2,1,0:T(8,128)S(1)} custom-call(s32[2,320]{1,0:T(2,128)S(1)} %bitcast.7, s32[1,1]{1,0:T(1,128)S(6)} %copy.7.count_ref, f32[320,128,128]{2,1,0:T(8,128)S(1)} %bitcast.5, f32[4,32,512]{2,1,0:T(8,128)S(1)} %gather_line.1.own_ref, f32[4,32,512]{2,1,0:T(8,128)S(1)} %collective-permute-done.10.came_ref, ...), custom_call_target="tpu_custom_call" | custom-call | flops 8053063680 | bytes 20971520 | tf_op jit(solution)/shard_map/transposed_product/pallas_call | solution.py:268
  26.4 0.4 %collective-permute-start.11 = (f32[32,512]{1,0:T(8,128)S(1)}, f32[32,512]{1,0:T(8,128)S(1)}, u32[]{:S(2)}, u32[]{:S(2)}) collective-permute-start(f32[32,512]{1,0:T(8,128)S(1)} %get-tuple-element.31), channel_id=1, source_target_pairs={{0,24},{8,16},{16,8},{24,0},{1,25},{9,17},{17,9},{25,1},{2,26},{10... | collective-permute-start | bytes 196616 | tf_op jit(solution)/shard_map/ppermute | solution.py:205
  26.7 2.8 %collective-permute-start.12 = (f32[32,512]{1,0:T(8,128)S(1)}, f32[32,512]{1,0:T(8,128)S(1)}, u32[]{:S(2)}, u32[]{:S(2)}) collective-permute-start(f32[32,512]{1,0:T(8,128)S(1)} %get-tuple-element.32), channel_id=1, source_target_pairs={{0,16},{8,24},{16,0},{24,8},{1,17},{9,25},{17,1},{25,9},{2,18},{10... | collective-permute-start | bytes 196616 | tf_op jit(solution)/shard_map/ppermute | solution.py:205
  29.6 0.0 collective-permute-done.7.refs_1_
  29.6 0.4 %collective-permute-start.13 = (f32[32,512]{1,0:T(8,128)S(1)}, f32[32,512]{1,0:T(8,128)S(1)}, u32[]{:S(2)}, u32[]{:S(2)}) collective-permute-start(f32[32,512]{1,0:T(8,128)S(1)} %get-tuple-element.33), channel_id=1, source_target_pairs={{0,8},{8,0},{16,24},{24,16},{1,9},{9,1},{17,25},{25,17},{2,10},{10... | collective-permute-start | bytes 196616 | tf_op jit(solution)/shard_map/ppermute | solution.py:205
  29.9 0.0 collective-permute-done.8.refs_2_
  29.9 0.0 collective-permute-done.9.refs_3_
  30.0 2.2 %collective-permute-done.11.refs_1_ = f32[32,512]{1,0:T(8,128)S(1)} collective-permute-done((f32[32,512]{1,0:T(8,128)S(1)}, f32[32,512]{1,0:T(8,128)S(1)}, u32[]{:S(2)}, u32[]{:S(2)}) %collective-permute-start.11) | collective-permute-done | bytes 65568 | tf_op jit(solution)/shard_map/ppermute | solution.py:205
  32.1 1.1 %collective-permute-done.12.refs_2_ = f32[32,512]{1,0:T(8,128)S(1)} collective-permute-done((f32[32,512]{1,0:T(8,128)S(1)}, f32[32,512]{1,0:T(8,128)S(1)}, u32[]{:S(2)}, u32[]{:S(2)}) %collective-permute-start.12) | collective-permute-done | bytes 65568 | tf_op jit(solution)/shard_map/ppermute | solution.py:205
  33.2 0.6 %collective-permute-done.13.refs_3_ = f32[32,512]{1,0:T(8,128)S(1)} collective-permute-done((f32[32,512]{1,0:T(8,128)S(1)}, f32[32,512]{1,0:T(8,128)S(1)}, u32[]{:S(2)}, u32[]{:S(2)}) %collective-permute-start.13) | collective-permute-done | bytes 65568 | tf_op jit(solution)/shard_map/ppermute | solution.py:205
  33.8 0.6 %sum_pieces.1 = (f32[16,512]{1,0:T(8,128)}, f32[16,512]{1,0:T(8,128)}) custom-call(f32[32,512]{1,0:T(8,128)S(1)} %sum_line.1.refs_0_, f32[32,512]{1,0:T(8,128)S(1)} %collective-permute-done.11.refs_1_, f32[32,512]{1,0:T(8,128)S(1)} %collective-permute-done.12.refs_2_, f32[32,512]{1,0:T(8,128)S(1)} %collective-permute-done.13.refs_3_), custom_call_target="tpu_custom_call" | custom-call | tf_op jit(solution)/shard_map/sum_pieces/pallas_call | solution.py:20
  (5 shorter events, 0.1 us)
Async XLA Ops:
  1.4 11.8 %copy-start = (f32[1,1,320,128,128]{4,3,2,1,0:T(8,128)S(1)}, f32[1,1,320,128,128]{4,3,2,1,0:T(8,128)}, u32[]{:S(2)}) copy-start(f32[1,1,320,128,128]{4,3,2,1,0:T(8,128)} %param.5) | copy-start | bytes 62914564
  1.4 11.8 %copy-start.1 = (s32[1,1,320,2]{2,3,1,0:T(2,128)S(1)}, s32[1,1,320,2]{2,3,1,0:T(2,128)}, u32[]{:S(2)}) copy-start(s32[1,1,320,2]{2,3,1,0:T(2,128)} %param.6) | copy-start | bytes 7684
  1.4 9.8 %collective-permute-start.5 = (f32[32,512]{1,0:T(8,128)S(1)}, f32[32,512]{1,0:T(8,128)S(1)}, u32[]{:S(2)}, u32[]{:S(2)}) collective-permute-start(f32[32,512]{1,0:T(8,128)S(1)} %own_share.1.refs_0_.refs_3_), channel_id=1, source_target_pairs={{0,24},{8,16},{16,8},{24,0},{1,25},{9,17},{17,9},{25,1},{2,26},{10... | collective-permute-start | bytes 196616 | tf_op jit(solution)/shard_map/ppermute | solution.py:205
  5.4 7.8 %collective-permute-start.4 = (f32[32,512]{1,0:T(8,128)S(1)}, f32[32,512]{1,0:T(8,128)S(1)}, u32[]{:S(2)}, u32[]{:S(2)}) collective-permute-start(f32[32,512]{1,0:T(8,128)S(1)} %own_share.1.refs_0_.refs_3_), channel_id=1, source_target_pairs={{0,16},{8,24},{16,0},{24,8},{1,17},{9,25},{17,1},{25,9},{2,18},{10... | collective-permute-start | bytes 196616 | tf_op jit(solution)/shard_map/ppermute | solution.py:205
  5.9 7.3 %collective-permute-start.3 = (f32[32,512]{1,0:T(8,128)S(1)}, f32[32,512]{1,0:T(8,128)S(1)}, u32[]{:S(2)}, u32[]{:S(2)}) collective-permute-start(f32[32,512]{1,0:T(8,128)S(1)} %own_share.1.refs_0_.refs_3_), channel_id=1, source_target_pairs={{0,8},{8,0},{16,24},{24,16},{1,9},{9,1},{17,25},{25,17},{2,10},{10... | collective-permute-start | bytes 196616 | tf_op jit(solution)/shard_map/ppermute | solution.py:205
  6.0 11.9 %collective-permute-start.2 = (f32[32,512]{1,0:T(8,128)S(1)}, f32[32,512]{1,0:T(8,128)S(1)}, u32[]{:S(2)}, u32[]{:S(2)}) collective-permute-start(f32[32,512]{1,0:T(8,128)S(1)} %own_share.1.refs_0_.refs_3_), channel_id=1, source_target_pairs={{0,2},{1,3},{2,4},{3,5},{4,6},{5,7},{6,0},{7,1},{8,10},{9,11},{10,... | collective-permute-start | bytes 196616 | tf_op jit(solution)/shard_map/ppermute | solution.py:210
  8.0 9.9 %collective-permute-start.1 = (f32[32,512]{1,0:T(8,128)S(1)}, f32[32,512]{1,0:T(8,128)S(1)}, u32[]{:S(2)}, u32[]{:S(2)}) collective-permute-start(f32[32,512]{1,0:T(8,128)S(1)} %own_share.1.refs_0_.refs_3_), channel_id=1, source_target_pairs={{0,4},{1,5},{2,6},{3,7},{4,0},{5,1},{6,2},{7,3},{8,12},{9,13},{10,... | collective-permute-start | bytes 196616 | tf_op jit(solution)/shard_map/ppermute | solution.py:210
  11.3 6.7 %collective-permute-start = (f32[32,512]{1,0:T(8,128)S(1)}, f32[32,512]{1,0:T(8,128)S(1)}, u32[]{:S(2)}, u32[]{:S(2)}) collective-permute-start(f32[32,512]{1,0:T(8,128)S(1)} %own_share.1.refs_0_.refs_3_), channel_id=1, source_target_pairs={{0,6},{1,7},{2,0},{3,1},{4,2},{5,3},{6,4},{7,5},{8,14},{9,15},{10,... | collective-permute-start | bytes 196616 | tf_op jit(solution)/shard_map/ppermute | solution.py:210
  18.3 1.6 %collective-permute-start.6 = (f32[4,32,512]{2,1,0:T(8,128)S(1)}, f32[4,32,512]{2,1,0:T(8,128)S(1)}, u32[]{:S(2)}, u32[]{:S(2)}) collective-permute-start(f32[4,32,512]{2,1,0:T(8,128)S(1)} %route_leaving.1), channel_id=1, source_target_pairs={{0,1},{1,0},{2,3},{3,2},{4,5},{5,4},{6,7},{7,6},{8,9},{9,8},{10,11... | collective-permute-start | bytes 786440 | tf_op jit(solution)/shard_map/ppermute | solution.py:205
  18.4 5.6 %collective-permute-start.10 = (f32[4,32,512]{2,1,0:T(8,128)S(1)}, f32[4,32,512]{2,1,0:T(8,128)S(1)}, u32[]{:S(2)}, u32[]{:S(2)}) collective-permute-start(f32[4,32,512]{2,1,0:T(8,128)S(1)} %gather_line.1.own_ref), channel_id=1, source_target_pairs={{0,1},{1,0},{2,3},{3,2},{4,5},{5,4},{6,7},{7,6},{8,9},{9,8},{10,11... | collective-permute-start | bytes 786440 | tf_op jit(solution)/shard_map/ppermute | solution.py:205
  19.9 9.6 %collective-permute-start.7 = (f32[32,512]{1,0:T(8,128)S(1)}, f32[32,512]{1,0:T(8,128)S(1)}, u32[]{:S(2)}, u32[]{:S(2)}) collective-permute-start(f32[32,512]{1,0:T(8,128)S(1)} %get-tuple-element.23), channel_id=1, source_target_pairs={{0,2},{1,3},{2,4},{3,5},{4,6},{5,7},{6,0},{7,1},{8,10},{9,11},{10,... | collective-permute-start | bytes 196616 | tf_op jit(solution)/shard_map/ppermute | solution.py:210
  21.5 8.4 %collective-permute-start.8 = (f32[32,512]{1,0:T(8,128)S(1)}, f32[32,512]{1,0:T(8,128)S(1)}, u32[]{:S(2)}, u32[]{:S(2)}) collective-permute-start(f32[32,512]{1,0:T(8,128)S(1)} %get-tuple-element.24), channel_id=1, source_target_pairs={{0,4},{1,5},{2,6},{3,7},{4,0},{5,1},{6,2},{7,3},{8,12},{9,13},{10,... | collective-permute-start | bytes 196616 | tf_op jit(solution)/shard_map/ppermute | solution.py:210
  23.0 7.0 %collective-permute-start.9 = (f32[32,512]{1,0:T(8,128)S(1)}, f32[32,512]{1,0:T(8,128)S(1)}, u32[]{:S(2)}, u32[]{:S(2)}) collective-permute-start(f32[32,512]{1,0:T(8,128)S(1)} %get-tuple-element.25), channel_id=1, source_target_pairs={{0,6},{1,7},{2,0},{3,1},{4,2},{5,3},{6,4},{7,5},{8,14},{9,15},{10,... | collective-permute-start | bytes 196616 | tf_op jit(solution)/shard_map/ppermute | solution.py:210
  26.4 5.7 %collective-permute-start.11 = (f32[32,512]{1,0:T(8,128)S(1)}, f32[32,512]{1,0:T(8,128)S(1)}, u32[]{:S(2)}, u32[]{:S(2)}) collective-permute-start(f32[32,512]{1,0:T(8,128)S(1)} %get-tuple-element.31), channel_id=1, source_target_pairs={{0,24},{8,16},{16,8},{24,0},{1,25},{9,17},{17,9},{25,1},{2,26},{10... | collective-permute-start | bytes 196616 | tf_op jit(solution)/shard_map/ppermute | solution.py:205
  26.7 6.4 %collective-permute-start.12 = (f32[32,512]{1,0:T(8,128)S(1)}, f32[32,512]{1,0:T(8,128)S(1)}, u32[]{:S(2)}, u32[]{:S(2)}) collective-permute-start(f32[32,512]{1,0:T(8,128)S(1)} %get-tuple-element.32), channel_id=1, source_target_pairs={{0,16},{8,24},{16,0},{24,8},{1,17},{9,25},{17,1},{25,9},{2,18},{10... | collective-permute-start | bytes 196616 | tf_op jit(solution)/shard_map/ppermute | solution.py:205
  29.6 4.3 %collective-permute-start.13 = (f32[32,512]{1,0:T(8,128)S(1)}, f32[32,512]{1,0:T(8,128)S(1)}, u32[]{:S(2)}, u32[]{:S(2)}) collective-permute-start(f32[32,512]{1,0:T(8,128)S(1)} %get-tuple-element.33), channel_id=1, source_target_pairs={{0,8},{8,0},{16,24},{24,16},{1,9},{9,1},{17,25},{25,17},{2,10},{10... | collective-permute-start | bytes 196616 | tf_op jit(solution)/shard_map/ppermute | solution.py:205
